TPU v7x, 32 devices: a whole 2x2x4 slice. The times are simulated.
32 devices in a mesh: req: 8 (over y, x, core), tp: 4 (over z).
Axes of the slice: x: 2, y: 2, z: 4, core: 2. Of those that a mesh axis runs over, the one named last changes fastest.
Arguments:
- activations: bfloat16 [2048, 2304], P('req'), may hold values from -6 to 6
- lengths: int32 [8, 4], P('req'), may hold values from 1 to 192, 256 in all within a row
- adapter_of: int32 [8, 4], P('req'), may hold values from 0 to 15
- slot_of: int32 [16], replicated, may hold values from 0 to 15, as said below
- page_table: int32 [8, 6], P('req'), may hold values from 0 to 5, each once within a row
- experts_of: int32 [2048, 2], P('req'), may hold values from 0 to 7, all different within a row; in each aligned block of 256 rows (0 to 255, 256 to 511, ...) at most 72 rows name the same one
- attn_gain: float32 [2304], replicated, may hold values from 0.25 to 1.75
- moe_gain: float32 [2304], replicated, may hold values from 0.25 to 1.75
- w_qkv: bfloat16 [2304, 3, 2304], P(None, None, 'tp'), may hold values from -4 to 4
- output_weight: bfloat16 [2304, 2304], P('tp'), may hold values from -0.125 to 0.125
- router: bfloat16 [2304, 8], replicated, may hold values from -0.125 to 0.125
- w_gate_up: bfloat16 [8, 2304, 2, 5760], P('req', None, None, 'tp'), may hold values from -0.125 to 0.125
- w_down: bfloat16 [8, 5760, 2304], P('req', 'tp'), may hold values from -0.078125 to 0.078125
- expert_up_factors: bfloat16 [8, 256, 2, 5760], P('req', None, None, 'tp'), may hold values from -0.59765625 to 0.59765625
- pool_a: bfloat16 [16, 2304, 64], P('req'), may hold values from -0.125 to 0.125
- slot_query_key_value_up: bfloat16 [16, 16, 3, 2304], P('req', None, None, 'tp'), may hold values from -0.59765625 to 0.59765625
- pool_aout: bfloat16 [16, 2304, 16], P('req', 'tp'), may hold values from -0.125 to 0.125
- pool_bout: bfloat16 [16, 16, 2304], P('req'), may hold values from -1.796875 to 1.796875
Outputs:
- layer_out: bfloat16 [2048, 2304], P('req')
- page_cache: bfloat16 [48, 128, 2, 2304], P('req', None, None, 'tp')
Inputs may be any that keep to these rules, and one draw needn't show every extreme that they name: `slot_of`: distinct slots. `page_table`: each row holds every page index once. `experts_of`: the two experts of a token differ; among the 256 tokens of one index of req at most 72 choose one expert, and some expert reaches 72.
All inputs are finite; a program needn't handle non-finite values.
Results may differ from a plain program's by a relative error of at most 0.0095.
Values may be sent and summed in bfloat16 or wider, within the bound.
A program may use at most 128 MiB of HBM per device.

v0:
```python
import math
import jax
import jax.numpy as jnp
from jax import lax
from jax.sharding import PartitionSpec as P

D = 2304
HEAD_SIZE = 64
EXPERTS = 8
ADAPTER_RANK = 16
ADAPTER_TOTAL = 16
PAGE = 128
CAP = 72
epsilon = 1e-05
adapter_scale = 2.0
rope_base = 10000.0


def rms_norm(values, scales):
    mean_sq = jnp.mean(values * values, axis=-1, keepdims=True)
    return values * lax.rsqrt(mean_sq + epsilon) * scales


def token_layout(lengths_row, tok_count):
    ends_at = jnp.cumsum(lengths_row)
    starts = ends_at - lengths_row
    places = jnp.arange(tok_count, dtype=jnp.int32)
    request = jnp.sum((places[:, None] >= ends_at[None, :]).astype(jnp.int32), axis=1)
    position = places - starts[request]
    return (request, position)


def rotate(values, position):
    head_dim = values.shape[-1]
    half_dim = head_dim // 2
    frequency = rope_base ** (-jnp.arange(half_dim, dtype=jnp.float32) * 2.0 / head_dim)
    angles = position.astype(jnp.float32)[:, None] * frequency[None, :]
    cosine = jnp.cos(angles)[:, None, :]
    sine_part = jnp.sin(angles)[:, None, :]
    front_half = values[..., :half_dim]
    back_half = values[..., half_dim:]
    return jnp.concatenate(
        [front_half * cosine - back_half * sine_part, back_half * cosine + front_half * sine_part],
        axis=-1,
    )


def per_device(
    activations,
    lengths,
    adapter_of,
    slot_of,
    page_table,
    experts_of,
    attn_gain,
    moe_gain,
    w_qkv,
    output_weight,
    router,
    w_gate_up,
    w_down,
    expert_up_factors,
    pool_a,
    slot_query_key_value_up,
    pool_aout,
    pool_bout,
):
    token_share = activations.shape[0]
    n_req = lax.axis_size("req")
    request, position = token_layout(lengths[0], token_share)
    adapter = adapter_of[0][request]
    token_slot = slot_of[adapter]
    pool_down, slot_up_factors, pool_head, pool_outup = (
        lax.all_gather(pool_a, "req", axis=0, tiled=True),
        lax.all_gather(slot_query_key_value_up, "req", axis=0, tiled=True),
        lax.all_gather(pool_aout, "req", axis=0, tiled=True),
        lax.all_gather(pool_bout, "req", axis=0, tiled=True),
    )
    slot_count = pool_down.shape[0]
    slot_hot = token_slot[:, None] == jnp.arange(slot_count, dtype=jnp.int32)[None, :]
    head_width = w_qkv.shape[2]
    heads_number = head_width // HEAD_SIZE
    normed = rms_norm(activations.astype(jnp.float32), attn_gain).astype(jnp.bfloat16)
    down_all = jnp.einsum(
        "td,sdr->tsr",
        normed,
        pool_down[:, :, : 3 * ADAPTER_RANK],
        preferred_element_type=jnp.float32,
    )
    coeff_qkv = jnp.sum(jnp.where(slot_hot[:, :, None], down_all, 0.0), axis=1).astype(jnp.bfloat16)
    spread_rows = jnp.where(
        slot_hot[:, :, None, None],
        coeff_qkv.reshape(token_share, 1, 3, ADAPTER_RANK),
        jnp.zeros((), jnp.bfloat16),
    )
    adapter_query_key_value = jnp.einsum(
        "qwxv,wvxd->qxd", spread_rows, slot_up_factors, preferred_element_type=jnp.float32
    )
    plain_query_key_value = jnp.dot(
        normed, w_qkv.reshape(D, 3 * head_width), preferred_element_type=jnp.float32
    ).reshape(token_share, 3, head_width)
    projection_result = (plain_query_key_value + adapter_scale * adapter_query_key_value).reshape(
        token_share, 3, heads_number, HEAD_SIZE
    )
    queries = rotate(projection_result[:, 0], position).astype(jnp.bfloat16)
    keys_roped = rotate(projection_result[:, 1], position).astype(jnp.bfloat16)
    values = projection_result[:, 2].astype(jnp.bfloat16)
    pool_dev = page_table.shape[1]
    pages_used = (lengths[0] + PAGE - 1) // PAGE
    first_page = jnp.cumsum(pages_used) - pages_used
    local_page = page_table[0][first_page[request] + position // PAGE]
    cache_row = local_page * PAGE + position % PAGE
    place_hot = (
        jnp.arange(pool_dev * PAGE, dtype=jnp.int32)[:, None] == cache_row[None, :]
    ).astype(jnp.bfloat16)
    key_value = jnp.stack(
        [keys_roped.reshape(token_share, head_width), values.reshape(token_share, head_width)],
        axis=1,
    ).reshape(token_share, 2 * head_width)
    page_cache = (
        jnp.dot(place_hot, key_value, preferred_element_type=jnp.float32)
        .astype(jnp.bfloat16)
        .reshape(pool_dev, PAGE, 2, head_width)
    )
    scores = jnp.einsum("qhd,khd->hqk", queries, keys_roped, preferred_element_type=jnp.float32) * (
        1.0 / math.sqrt(HEAD_SIZE)
    )
    allowed = (request[:, None] == request[None, :]) & (position[None, :] <= position[:, None])
    scores = jnp.where(allowed[None], scores, -1e30)
    row_max = jnp.max(scores, axis=-1, keepdims=True)
    weights = jnp.exp(scores - row_max)
    weights = (weights / jnp.sum(weights, axis=-1, keepdims=True)).astype(jnp.bfloat16)
    attention_result = (
        jnp.einsum("hqk,khd->qhd", weights, values, preferred_element_type=jnp.float32)
        .astype(jnp.bfloat16)
        .reshape(token_share, head_width)
    )
    aout_all = jnp.einsum(
        "tc,scr->tsr", attention_result, pool_head, preferred_element_type=jnp.float32
    )
    coeff_out = jnp.sum(jnp.where(slot_hot[:, :, None], aout_all, 0.0), axis=1)
    spread_out = jnp.where(slot_hot[:, :, None], coeff_out[:, None, :], 0.0).reshape(
        token_share, slot_count * ADAPTER_RANK
    )
    output_update = jnp.dot(
        spread_out,
        pool_outup.astype(jnp.float32).reshape(slot_count * ADAPTER_RANK, D),
        precision=lax.Precision.HIGHEST,
    )
    head_term = (
        jnp.dot(attention_result, output_weight, preferred_element_type=jnp.float32)
        + adapter_scale * output_update
    )
    mixed_out = lax.psum(head_term, "tp")
    residual_stream = activations.astype(jnp.float32) + mixed_out
    normed_moe = rms_norm(residual_stream, moe_gain).astype(jnp.bfloat16)
    logits = jnp.dot(normed_moe, router, preferred_element_type=jnp.float32)
    chosen = jnp.take_along_axis(logits, experts_of, axis=1)
    gate_weights = 1.0 / (1.0 + jnp.exp(chosen[:, ::-1] - chosen))
    exp_all = jnp.einsum(
        "td,sdr->tsr",
        normed_moe,
        pool_down[:, :, 3 * ADAPTER_RANK :],
        preferred_element_type=jnp.float32,
    )
    coeff_exp = jnp.sum(jnp.where(slot_hot[:, :, None], exp_all, 0.0), axis=1).astype(jnp.bfloat16)
    capacity = CAP
    split_count = n_req // EXPERTS
    flat_expert = experts_of.reshape(-1)
    expert_hot = (flat_expert[:, None] == jnp.arange(EXPERTS, dtype=jnp.int32)[None, :]).astype(
        jnp.int32
    )
    order_in = jnp.sum((jnp.cumsum(expert_hot, axis=0) - expert_hot) * expert_hot, axis=1)
    column = flat_expert * capacity + order_in
    pick = (column[:, None] == jnp.arange(EXPERTS * capacity, dtype=jnp.int32)[None, :]).reshape(
        token_share, 2, EXPERTS * capacity
    )
    route = jnp.any(pick, axis=1).astype(jnp.bfloat16)
    combine_weights = jnp.sum(jnp.where(pick, gate_weights[:, :, None], 0.0), axis=1)

    def spread_copies(array):
        shaped = array.reshape((EXPERTS, 1, capacity) + array.shape[1:])
        return jnp.broadcast_to(shaped, (EXPERTS, split_count, capacity) + array.shape[1:]).reshape(
            (n_req, capacity) + array.shape[1:]
        )

    send_coeff = jnp.einsum(
        "ts,tr->sr", route, coeff_exp, preferred_element_type=jnp.float32
    ).astype(jnp.bfloat16)
    send_ids = jnp.einsum(
        "ts,t->s", route, adapter.astype(jnp.bfloat16), preferred_element_type=jnp.float32
    ).astype(jnp.bfloat16)
    adapter_range = jnp.arange(ADAPTER_TOTAL, dtype=jnp.int32).astype(jnp.bfloat16)
    send_rows = jnp.einsum(
        "ts,td->sd", route, normed_moe, preferred_element_type=jnp.float32
    ).astype(jnp.bfloat16)
    expert_input_rows = lax.all_to_all(
        spread_copies(send_rows), "req", split_axis=0, concat_axis=0, tiled=True
    )
    coeff_rank = lax.all_to_all(
        spread_copies(send_coeff), "req", split_axis=0, concat_axis=0, tiled=True
    )
    adapter_ids = lax.all_to_all(
        spread_copies(send_ids), "req", split_axis=0, concat_axis=0, tiled=True
    )
    count = expert_input_rows.shape[1]
    flat_rows = expert_input_rows.reshape(n_req * count, D)
    flat_coeff = coeff_rank.reshape(n_req * count, ADAPTER_RANK)
    flat_ids = adapter_ids.reshape(n_req * count)
    unit_count = w_gate_up.shape[3]
    broad_coefficients = jnp.where(
        flat_ids[:, None, None] == adapter_range[None, :, None],
        flat_coeff[:, None, :],
        jnp.zeros((), jnp.bfloat16),
    ).reshape(n_req * count, ADAPTER_TOTAL * ADAPTER_RANK)
    before_norm = jnp.dot(
        flat_rows, w_gate_up[0].reshape(D, 2 * unit_count), preferred_element_type=jnp.float32
    )
    before_norm = before_norm + adapter_scale * jnp.dot(
        broad_coefficients,
        expert_up_factors[0].reshape(ADAPTER_TOTAL * ADAPTER_RANK, 2 * unit_count),
        preferred_element_type=jnp.float32,
    )
    hidden = (jax.nn.silu(before_norm[:, :unit_count]) * before_norm[:, unit_count:]).astype(
        jnp.bfloat16
    )
    partial_term = jnp.dot(hidden, w_down[0], preferred_element_type=jnp.float32).astype(
        jnp.bfloat16
    )
    returned = lax.all_to_all(
        partial_term.reshape(n_req, count, D), "req", split_axis=0, concat_axis=0, tiled=True
    )
    summed = jnp.sum(
        returned.astype(jnp.float32).reshape(EXPERTS, split_count, capacity, D), axis=1
    ).reshape(EXPERTS * capacity, D)
    moe_part = jnp.dot(combine_weights, summed, precision=lax.Precision.HIGHEST)
    moe_sum = lax.psum(moe_part.astype(jnp.bfloat16), "tp").astype(jnp.float32)
    layer_out = (residual_stream + moe_sum).astype(jnp.bfloat16)
    return (layer_out, page_cache)


def solution(mesh):
    return jax.shard_map(
        per_device,
        mesh=mesh,
        in_specs=(
            P("req", None),
            P("req", None),
            P("req", None),
            P(),
            P("req", None),
            P("req", None),
            P(),
            P(),
            P(None, None, "tp"),
            P("tp", None),
            P(),
            P("req", None, None, "tp"),
            P("req", "tp", None),
            P("req", None, None, "tp"),
            P("req", None, None),
            P("req", None, None, "tp"),
            P("req", "tp", None),
            P("req", None, None),
        ),
        out_specs=(P("req", None), P("req", None, None, "tp")),
        check_vma=False,
    )
```

profile of v0, /device:TPU:0, one launch (start us, length us, event | category | flops | bytes accessed | tf_op | source)
XLA Modules:
  0.0 364.0 jit_solution(4491412793175182737)
XLA Ops:
  11.3 1.6 fusion.10
  12.9 1.5 fusion.63
  14.3 1.5 fusion.66
  15.8 2.0 fusion.62
  17.8 6.8 %compare_select_fusion.9 = (s32[256,1]{0,1:T(1,128)S(1)}, s32[256,1]{0,1:T(1,128)S(1)}, s32[256,1]{0,1:T(1,128)S(1)}) fusion(s32[]{:T(128)} %bitcast.20, s32[]{:T(128)} %bitcast.21, s32[]{:T(128)} %bitcast.22, s32[]{:T(128)} %bitcast.23, s32[]{:T(128)} %bitcast.24, s32[]{:T(128)} %bitcast.26, s32[]{:T(128)} %bitcast.25, s32[]{:T(128)} %bitcast.10, ...), kind=kLoop, calls=%fused_computation.105 | loop fusion | flops 6144 | bytes 4140 | tf_op jit(solution)/shard_map/gather | solution.py:72
  24.6 5.7 %select_select_fusion.2 = s32[256]{0:T(256)S(1)} fusion(pred[256]{0:T(512)(128)(4,1)S(1)} %get-tuple-element.22, pred[256]{0:T(512)(128)(4,1)S(1)} %get-tuple-element.21, pred[256]{0:T(512)(128)(4,1)S(1)} %get-tuple-element.20, pred[256]{0:T(512)(128)(4,1)S(1)} %get-tuple-element.19, pred[256]{0:T(512)(128)(4,1)S(1)} %get-tuple-element.18, ...), kind=kLoop, calls=%fused_computation.137 | loop fusion | flops 2304 | bytes 4388 | tf_op jit(solution)/shard_map/gather | solution.py:72
  31.0 8.8 %fusion.49 = (s32[256,1]{0,1:T(1,128)S(1)}, s32[256,1]{0,1:T(1,128)S(1)}) fusion(s32[]{:T(128)} %bitcast.71, s32[]{:T(128)} %bitcast.72, s32[]{:T(128)} %bitcast.73, s32[]{:T(128)} %bitcast.67, s32[]{:T(128)} %bitcast.74, s32[]{:T(128)} %bitcast.68, s32[]{:T(128)} %bitcast.76, s32[]{:T(128)} %bitcast.75, s32[]{:T(128)} %bitcast.70, s32[]{:T(128)} %bitcast.69, ...), kind=kLoop, calls=%fused_computation.132 | loop fusion | flops 11008 | bytes 3128 | tf_op jit(solution)/shard_map/mul | solution.py:112
  40.0 12.0 %all_gather.14 = bf16[16,576,16]{1,2,0:T(8,128)(2,1)S(1)} all-gather(bf16[2,576,16]{1,2,0:T(8,128)(2,1)} %param.34), channel_id=1, replica_groups=mesh['req'=8,'tp'=4] {'req'}, dimensions={0}, use_global_device_ids=true | all-gather | bytes 331776 | tf_op jit(solution)/shard_map/all_gather | solution.py:76
  52.0 12.0 %all_gather.13 = bf16[16,16,3,576]{3,1,2,0:T(8,128)(2,1)} all-gather(bf16[2,16,3,576]{3,1,2,0:T(8,128)(2,1)S(1)} %copy-done.14), channel_id=1, replica_groups=mesh['req'=8,'tp'=4] {'req'}, dimensions={0}, use_global_device_ids=true | all-gather | bytes 995328 | tf_op jit(solution)/shard_map/all_gather | solution.py:75
  64.2 6.8 %fusion.1 = f32[256,3,576]{0,2,1:T(8,128)} fusion(bf16[2304,3,576]{0,2,1:T(8,128)(2,1)} %param.26, bf16[256,2304]{1,0:T(8,128)(2,1)S(1)} %copy-done.5, f32[2304]{0:T(1024)S(1)} %copy-done.18, f32[256]{0:T(256)S(1)} %add_rsqrt_fusion.1), kind=kOutput, calls=%fused_computation.2 | convolution fusion | flops 2040791040 | bytes 10921984 | tf_op jit(solution)/shard_map/dot_general | solution.py:99
  71.0 1.5 copy-done.6
  78.1 3.4 fusion.67
  81.5 2.2 convolution_convert_fusion.3
  84.1 2.5 fusion.8
  86.5 2.6 convolution_add_fusion
  93.1 3.4 all-to-all-start.1
  96.6 88.4 %all-reduce.3.cloned.1.call-done = f32[256,2304]{1,0:T(8,128)} async-done(((f32[256,2304]{1,0:T(8,128)}), f32[256,2304]{1,0:T(8,128)}) %all-reduce.3.cloned.1.call-update) | async-done | bytes 2359312 | tf_op jit(solution)/shard_map/psum | solution.py:154
  185.0 2.5 multiply_reduce_fusion
  190.9 3.7 %all-to-all-start.2 = ((bf16[8,72,16]{1,2,0:T(8,128)(2,1)}), bf16[8,72,16]{1,2,0:T(8,128)(2,1)S(1)}, u32[]{:S(2)}, u32[]{:S(2)}) async-start(bf16[8,72,16]{1,2,0:T(8,128)(2,1)} %copy.92), calls=%async_computation.2 | async-start | bytes 65536 | tf_op jit(solution)/shard_map/all_to_all | solution.py:200
  194.6 3.7 %convolution_convert_fusion = bf16[576,2304]{1,0:T(8,128)(2,1)} fusion(pred[256,576]{0,1:T(8,128)(4,1)S(1)} %fusion.17, bf16[256,2304]{1,0:T(8,128)(2,1)} %copy-done.3), kind=kOutput, calls=%fused_computation.8 | convolution fusion | flops 680804352 | bytes 3981312 | tf_op jit(solution)/shard_map/ts,td->sd/dot_general | solution.py:194
  199.4 3.6 all-to-all-start
  203.5 32.1 %all-to-all-done = bf16[8,72,2304]{2,1,0:T(8,128)(2,1)S(1)} async-done(((bf16[8,72,2304]{2,1,0:T(8,128)(2,1)}), bf16[8,72,2304]{2,1,0:T(8,128)(2,1)S(1)}, u32[]{:S(2)}, u32[]{:S(2)}) %all-to-all-start) | async-done | bytes 2654240 | tf_op jit(solution)/shard_map/all_to_all | solution.py:197
  235.6 11.4 %fusion.72 = f32[576,2880]{1,0:T(8,128)S(1)} fusion(bf16[576,2304]{1,0:T(8,128)(2,1)S(1)} %bitcast.153, bf16[2304,2880]{0,1:T(8,128)(2,1)} %bitcast.173), kind=kOutput, calls=%fused_computation.165 | convolution fusion | flops 7644119040 | bytes 22560768 | tf_op jit(solution)/shard_map/dot_general | solution.py:216
  248.3 9.2 %fusion.5 = bf16[576,2304]{1,0:T(8,128)(2,1)} fusion(bf16[1,1440,2304]{2,1,0:T(8,128)(2,1)} %param.30, f32[576,2880]{1,0:T(8,128)S(1)} %multiply_add_fusion), kind=kOutput, calls=%fused_computation.7 | convolution fusion | flops 3828363264 | bytes 16367616 | tf_op jit(solution)/shard_map/dot_general | solution.py:227
  257.5 4.5 %all-to-all-start.3 = ((bf16[8,72,2304]{2,1,0:T(8,128)(2,1)}), bf16[8,72,2304]{2,1,0:T(8,128)(2,1)}, u32[]{:S(2)}, u32[]{:S(2)}) async-start(bf16[8,72,2304]{2,1,0:T(8,128)(2,1)} %bitcast.152), calls=%async_computation.3 | async-start | bytes 5308416 | tf_op jit(solution)/shard_map/all_to_all | solution.py:230
  263.0 3.6 gather_fusion
  267.1 27.5 %all-to-all-done.3 = bf16[8,72,2304]{2,1,0:T(8,128)(2,1)} async-done(((bf16[8,72,2304]{2,1,0:T(8,128)(2,1)}), bf16[8,72,2304]{2,1,0:T(8,128)(2,1)}, u32[]{:S(2)}, u32[]{:S(2)}) %all-to-all-start.3) | async-done | bytes 2654240 | tf_op jit(solution)/shard_map/all_to_all | solution.py:230
  294.6 5.9 %convolution_convert_fusion.1 = bf16[256,2304]{1,0:T(8,128)(2,1)} fusion(f32[256,576]{0,1:T(8,128)S(1)} %select_reduce_fusion, bf16[576,2304]{1,0:T(8,128)(2,1)} %bitcast.65), kind=kOutput, calls=%fused_computation.12 | convolution fusion | flops 4077453312 | bytes 4423680 | tf_op jit(solution)/shard_map/dot_general | solution.py:236
  302.5 3.0 reshape.581
  305.5 6.7 %copy.94 = bf16[6,128,2,576]{1,3,2,0:T(8,128)(2,1)} copy(bf16[6,128,2,576]{3,2,1,0:T(2,128)(2,1)} %reshape.581) | data formatting | bytes 3538944
  312.2 41.7 %all-reduce.5.cloned.1.call-done = bf16[256,2304]{1,0:T(8,128)(2,1)} async-done(((bf16[256,2304]{1,0:T(8,128)(2,1)}), bf16[256,2304]{1,0:T(8,128)(2,1)}) %all-reduce.5.cloned.1.call-update) | async-done | bytes 1179664 | tf_op jit(solution)/shard_map/psum | solution.py:237
  353.8 3.7 %add_convert_fusion = bf16[256,2304]{1,0:T(8,128)(2,1)} fusion(bf16[256,2304]{1,0:T(8,128)(2,1)} %all-reduce.5.cloned.1.call-done, f32[256,2304]{1,0:T(8,128)} %all-reduce.3.cloned.1.call-done, bf16[256,2304]{1,0:T(8,128)(2,1)} %param.18), kind=kLoop, calls=%fused_computation.22 | loop fusion | flops 2949120 | bytes 5898240 | tf_op jit(solution)/shard_map/convert_element_type | solution.py:238
  (118 shorter events, 24.6 us)
Async XLA Ops:
  7.2 79.4 %copy-start = (bf16[576,2304]{1,0:T(8,128)(2,1)S(1)}, bf16[576,2304]{1,0:T(8,128)(2,1)}, u32[]{:S(2)}) copy-start(bf16[576,2304]{1,0:T(8,128)(2,1)} %param.27) | copy-start | bytes 7962628
  7.2 44.8 %copy-start.14 = (bf16[2,16,3,576]{3,1,2,0:T(8,128)(2,1)S(1)}, bf16[2,16,3,576]{3,1,2,0:T(8,128)(2,1)}, u32[]{:S(2)}) copy-start(bf16[2,16,3,576]{3,1,2,0:T(8,128)(2,1)} %param.33) | copy-start | bytes 331780
  7.2 57.0 %copy-start.18 = (f32[2304]{0:T(1024)S(1)}, f32[2304]{0:T(1024)}, u32[]{:S(2)}) copy-start(f32[2304]{0:T(1024)} %param.24) | copy-start | bytes 27652
  7.2 63.8 %all-gather.3.cloned.1.call-start = ((), (), s32[]{:S(2)}) async-start(), calls=%async_computation.4 | async-start | bytes 5308416 | tf_op jit(solution)/shard_map/all_gather | solution.py:74
  7.9 76.1 %all-gather.5.cloned.1.call-start = ((), (), s32[]{:S(2)}) async-start(), calls=%async_computation.5 | async-start | bytes 1327104 | tf_op jit(solution)/shard_map/all_gather | solution.py:77
  8.7 176.3 %all-reduce.3.cloned.1.call-start = ((), (), s32[]{:S(2)}) async-start(), calls=%async_computation.6 | async-start | bytes 4718592 | tf_op jit(solution)/shard_map/psum | solution.py:154
  10.4 53.8 %copy-start.5 = (bf16[256,2304]{1,0:T(8,128)(2,1)S(1)}, bf16[256,2304]{1,0:T(8,128)(2,1)}, u32[]{:S(2)}) copy-start(bf16[256,2304]{1,0:T(8,128)(2,1)} %param.18) | copy-start | bytes 3538948
  71.0 1.5 copy-start.6
  71.0 2.5 slice-start
  73.6 1.3 copy-start.9
  73.6 1.8 copy-start.10
  75.9 1.2 copy-start.8
  78.1 3.4 copy-start.12
  89.2 0.7 copy-start.16
  93.1 97.8 %all-to-all-start.1 = ((bf16[8,1,72]{2,1,0:T(2,128)(2,1)}), bf16[8,1,72]{2,1,0:T(2,128)(2,1)S(1)}, u32[]{:S(2)}, u32[]{:S(2)}) async-start(bf16[8,1,72]{2,1,0:T(2,128)(2,1)} %all_to_all.20), calls=%async_computation.1 | async-start | bytes 8192 | tf_op jit(solution)/shard_map/all_to_all | solution.py:203
  96.6 90.9 %copy-start.17 = (f32[2304]{0:T(1024)S(1)}, f32[2304]{0:T(1024)}, u32[]{:S(2)}) copy-start(f32[2304]{0:T(1024)} %param.25) | copy-start | bytes 27652
  185.0 2.7 copy-start.2
  185.0 3.0 copy-start.7
  188.0 1.5 slice-start.1
  188.4 1.0 copy-start.3
  190.9 8.5 %all-to-all-start.2 = ((bf16[8,72,16]{1,2,0:T(8,128)(2,1)}), bf16[8,72,16]{1,2,0:T(8,128)(2,1)S(1)}, u32[]{:S(2)}, u32[]{:S(2)}) async-start(bf16[8,72,16]{1,2,0:T(8,128)(2,1)} %copy.92), calls=%async_computation.2 | async-start | bytes 65536 | tf_op jit(solution)/shard_map/all_to_all | solution.py:200
  199.4 36.2 %all-to-all-start = ((bf16[8,72,2304]{2,1,0:T(8,128)(2,1)}), bf16[8,72,2304]{2,1,0:T(8,128)(2,1)S(1)}, u32[]{:S(2)}, u32[]{:S(2)}) async-start(bf16[8,72,2304]{2,1,0:T(8,128)(2,1)} %bitcast.55), calls=%async_computation | async-start | bytes 5308416 | tf_op jit(solution)/shard_map/all_to_all | solution.py:197
  235.6 11.4 %copy-start.11 = (bf16[1,256,2,1440]{1,3,2,0:T(8,128)(2,1)S(1)}, bf16[1,256,2,1440]{1,3,2,0:T(8,128)(2,1)}, u32[]{:S(2)}) copy-start(bf16[1,256,2,1440]{1,3,2,0:T(8,128)(2,1)} %param.31) | copy-start | bytes 4423684
  257.5 5.1 %copy-start.4 = (bf16[256,2304]{1,0:T(8,128)(2,1)S(1)}, bf16[256,2304]{1,0:T(8,128)(2,1)}, u32[]{:S(2)}) copy-start(bf16[256,2304]{1,0:T(8,128)(2,1)} %copy-done.3) | copy-start | bytes 3538948
  257.5 5.1 %copy-start.15 = (bf16[2304,8]{0,1:T(8,128)(2,1)S(1)}, bf16[2304,8]{0,1:T(8,128)(2,1)}, u32[]{:S(2)}) copy-start(bf16[2304,8]{0,1:T(8,128)(2,1)} %param.28) | copy-start | bytes 110596
  257.5 37.1 %all-to-all-start.3 = ((bf16[8,72,2304]{2,1,0:T(8,128)(2,1)}), bf16[8,72,2304]{2,1,0:T(8,128)(2,1)}, u32[]{:S(2)}, u32[]{:S(2)}) async-start(bf16[8,72,2304]{2,1,0:T(8,128)(2,1)} %bitcast.152), calls=%async_computation.3 | async-start | bytes 5308416 | tf_op jit(solution)/shard_map/all_to_all | solution.py:230
  262.0 91.8 %all-reduce.5.cloned.1.call-start = ((), (), s32[]{:S(2)}) async-start(), calls=%async_computation.7 | async-start | bytes 2359296 | tf_op jit(solution)/shard_map/psum | solution.py:237
  294.6 7.0 %copy-start.13 = (bf16[256,9,32]{0,2,1:T(8,128)(2,1)S(1)}, bf16[256,9,32]{0,2,1:T(8,128)(2,1)}, u32[]{:S(2)}) copy-start(bf16[256,9,32]{0,2,1:T(8,128)(2,1)} %copy-done.12) | copy-start | bytes 442372
  305.5 52.0 %copy-start.1 = (bf16[576,2304]{1,0:T(8,128)(2,1)S(1)}, bf16[576,2304]{1,0:T(8,128)(2,1)}, u32[]{:S(2)}) copy-start(bf16[576,2304]{1,0:T(8,128)(2,1)} %param.27) | copy-start | bytes 7962628
Sparse Core Ops, SparseCore 0:
  9.9 42.8 all-gather.2
  54.7 24.0 all-gather.4
  89.3 95.5 all-reduce.2
  300.6 53.1 all-reduce.4
where the time goes:
time: 365 us; the launch traced here: 364 us
  waiting for transfers between devices  192 us (53%)
  matrix products  52.9 us (14%)
  other arithmetic  35.5 us (10%)
  local copies, waits for them, and re-layouts  29.5 us (8%)
  blocking collectives  24 us (7%)
  starting transfers between devices  15.6 us (4%)
  between operations  14.2 us (4%)
    psum x1, waiting for transfers between devices, per_device(): mixed_out = lax.psum(head_term, 'tp')  88.4 us
    psum x1, waiting for transfers between devices, per_device(): moe_sum = lax.psum(moe_part.astype(jnp.bfloat16), 'tp').astype(jnp.float32)  41.7 us
    all_to_all x1, waiting for transfers between devices, per_device(): lax.all_to_all(spread_copies(send_rows), 'req', split_axis=0, concat_axis...  32.1 us
    all_to_all x1, waiting for transfers between devices, per_device(): lax.all_to_all(partial_term.reshape(n_req, count, D), 'req', split_axis=0...  27.5 us
    gather x3, other arithmetic, per_device(): token_slot = slot_of[adapter]  12.5 us
    unnamed x40, local copies, waits for them, and re-layouts  12.2 us
    all_gather x1, blocking collectives, per_device(): lax.all_gather(pool_aout, 'req', axis=0, tiled=True)  12 us
    all_gather x1, blocking collectives, per_device(): lax.all_gather(slot_query_key_value_up, 'req', axis=0, tiled=True)  12 us
  transfers between devices with their start and end apart: 8, of which 5 were waited for; matrix products, arithmetic and copies ran while one was open for 20% of the time, Pallas kernels for 0%

commit v1 on v0

--- a/solution.py
+++ b/solution.py
@@ -1,3 +1,4 @@
+import functools
 import math
 import jax
 import jax.numpy as jnp
@@ -14,6 +15,13 @@
 epsilon = 1e-05
 adapter_scale = 2.0
 rope_base = 10000.0
+
+
+def panels_advance(shard_in, peer_axis):
+    return jnp.sum(lax.all_gather(shard_in, peer_axis), axis=0)
+
+
+stops_all_guide = functools.partial(panels_advance, peer_axis="tp")
 
 
 def rms_norm(values, scales):
@@ -151,7 +159,7 @@
         jnp.dot(attention_result, output_weight, preferred_element_type=jnp.float32)
         + adapter_scale * output_update
     )
-    mixed_out = lax.psum(head_term, "tp")
+    mixed_out = stops_all_guide(head_term)
     residual_stream = activations.astype(jnp.float32) + mixed_out
     normed_moe = rms_norm(residual_stream, moe_gain).astype(jnp.bfloat16)
     logits = jnp.dot(normed_moe, router, preferred_element_type=jnp.float32)

time: 365 us -> 440 us (1.21)
  waiting for transfers between devices: 192 us -> 263 us
  other arithmetic: 35.5 us -> 40 us
    all_gather x0 -> x1, waiting for transfers between devices: none -> 159 us  [panels_advance(): return jnp.sum(lax.all_gather(shard_in, peer_axis), axis=0)]
    psum x1 -> x0, waiting for transfers between devices: 88.4 us -> none  [per_device(): mixed_out = lax.psum(head_term, 'tp')]
    reduce_sum x0 -> x1, other arithmetic: none -> 4.53 us  [panels_advance(): return jnp.sum(lax.all_gather(shard_in, peer_axis), axis=0)]
  transfers between devices with their start and end apart: 8 -> 8, of which waited for: 5 -> 5; matrix products, arithmetic and copies ran while one was open for 20% -> 18% of each run, Pallas kernels for 0% -> 0%
where the time goes in v1:
time: 440 us; the launch traced here: 438 us
  waiting for transfers between devices  263 us (60%)
  matrix products  52.8 us (12%)
  other arithmetic  40 us (9%)
  local copies, waits for them, and re-layouts  29 us (7%)
  blocking collectives  24 us (5%)
  starting transfers between devices  15.7 us (4%)
  between operations  14.3 us (3%)
    all_gather x1, waiting for transfers between devices, panels_advance(): return jnp.sum(lax.all_gather(shard_in, peer_axis), axis=0)  159 us
    psum x1, waiting for transfers between devices, per_device(): moe_sum = lax.psum(moe_part.astype(jnp.bfloat16), 'tp').astype(jnp.float32)  40.8 us
    all_to_all x1, waiting for transfers between devices, per_device(): lax.all_to_all(spread_copies(send_rows), 'req', split_axis=0, concat_axis...  32.1 us
    all_to_all x1, waiting for transfers between devices, per_device(): lax.all_to_all(partial_term.reshape(n_req, count, D), 'req', split_axis=0...  27.5 us
    gather x3, other arithmetic, per_device(): token_slot = slot_of[adapter]  12.5 us
    all_gather x1, blocking collectives, per_device(): lax.all_gather(pool_aout, 'req', axis=0, tiled=True)  12.1 us
    all_gather x1, blocking collectives, per_device(): lax.all_gather(slot_query_key_value_up, 'req', axis=0, tiled=True)  11.9 us
    unnamed x40, local copies, waits for them, and re-layouts  11.6 us
  transfers between devices with their start and end apart: 8, of which 5 were waited for; matrix products, arithmetic and copies ran while one was open for 18% of the time, Pallas kernels for 0%

profile of v1, /device:TPU:0, one launch (start us, length us, event | category | flops | bytes accessed | tf_op | source)
XLA Modules:
  0.0 438.3 jit_solution(7538993669030255398)
XLA Ops:
  11.3 1.6 fusion.10
  12.9 1.4 fusion.63
  14.3 1.6 fusion.66
  15.8 1.9 fusion.62
  17.8 6.8 %compare_select_fusion.9 = (s32[256,1]{0,1:T(1,128)S(1)}, s32[256,1]{0,1:T(1,128)S(1)}, s32[256,1]{0,1:T(1,128)S(1)}) fusion(s32[]{:T(128)} %bitcast.20, s32[]{:T(128)} %bitcast.21, s32[]{:T(128)} %bitcast.22, s32[]{:T(128)} %bitcast.23, s32[]{:T(128)} %bitcast.24, s32[]{:T(128)} %bitcast.26, s32[]{:T(128)} %bitcast.25, s32[]{:T(128)} %bitcast.10, ...), kind=kLoop, calls=%fused_computation.105 | loop fusion | flops 6144 | bytes 4140 | tf_op jit(solution)/shard_map/gather | solution.py:80
  24.7 5.6 %select_select_fusion.2 = s32[256]{0:T(256)S(1)} fusion(pred[256]{0:T(512)(128)(4,1)S(1)} %get-tuple-element.22, pred[256]{0:T(512)(128)(4,1)S(1)} %get-tuple-element.21, pred[256]{0:T(512)(128)(4,1)S(1)} %get-tuple-element.20, pred[256]{0:T(512)(128)(4,1)S(1)} %get-tuple-element.19, pred[256]{0:T(512)(128)(4,1)S(1)} %get-tuple-element.18, ...), kind=kLoop, calls=%fused_computation.137 | loop fusion | flops 2304 | bytes 4388 | tf_op jit(solution)/shard_map/gather | solution.py:80
  31.0 8.8 %fusion.49 = (s32[256,1]{0,1:T(1,128)S(1)}, s32[256,1]{0,1:T(1,128)S(1)}) fusion(s32[]{:T(128)} %bitcast.72, s32[]{:T(128)} %bitcast.73, s32[]{:T(128)} %bitcast.74, s32[]{:T(128)} %bitcast.68, s32[]{:T(128)} %bitcast.75, s32[]{:T(128)} %bitcast.69, s32[]{:T(128)} %bitcast.77, s32[]{:T(128)} %bitcast.76, s32[]{:T(128)} %bitcast.71, s32[]{:T(128)} %bitcast.70, ...), kind=kLoop, calls=%fused_computation.132 | loop fusion | flops 11008 | bytes 3128 | tf_op jit(solution)/shard_map/mul | solution.py:120
  39.9 12.1 %all_gather.20 = bf16[16,576,16]{1,2,0:T(8,128)(2,1)S(1)} all-gather(bf16[2,576,16]{1,2,0:T(8,128)(2,1)} %param.34), channel_id=1, replica_groups=mesh['req'=8,'tp'=4] {'req'}, dimensions={0}, use_global_device_ids=true | all-gather | bytes 331776 | tf_op jit(solution)/shard_map/all_gather | solution.py:84
  52.0 11.9 %all_gather.19 = bf16[16,16,3,576]{3,1,2,0:T(8,128)(2,1)} all-gather(bf16[2,16,3,576]{3,1,2,0:T(8,128)(2,1)S(1)} %copy-done.14), channel_id=1, replica_groups=mesh['req'=8,'tp'=4] {'req'}, dimensions={0}, use_global_device_ids=true | all-gather | bytes 995328 | tf_op jit(solution)/shard_map/all_gather | solution.py:83
  64.1 6.8 %fusion.1 = f32[256,3,576]{0,2,1:T(8,128)} fusion(bf16[2304,3,576]{0,2,1:T(8,128)(2,1)} %param.26, bf16[256,2304]{1,0:T(8,128)(2,1)S(1)} %copy-done.5, f32[2304]{0:T(1024)S(1)} %copy-done.18, f32[256]{0:T(256)S(1)} %add_rsqrt_fusion.1), kind=kOutput, calls=%fused_computation.2 | convolution fusion | flops 2040791040 | bytes 10921984 | tf_op jit(solution)/shard_map/dot_general | solution.py:107
  78.0 3.4 fusion.67
  81.4 2.2 convolution_convert_fusion.3
  83.9 2.5 fusion.8
  86.4 2.5 convolution_add_fusion
  92.9 3.5 all-to-all-start.1
  96.5 159.5 %all-gather.9.cloned.1.call-done = f32[1024,2304]{1,0:T(8,128)} async-done(((f32[256,2304]{1,0:T(8,128)}), f32[1024,2304]{1,0:T(8,128)}) %all-gather.9.cloned.1.call-update) | async-done | bytes 9437200 | tf_op jit(solution)/shard_map/all_gather | solution.py:21
  255.9 4.5 %reduce_sum.104 = f32[256,2304]{1,0:T(8,128)S(1)} reduce(f32[4,256,2304]{2,1,0:T(8,128)} %bitcast.148, f32[]{:T(128)} %constant.84.clone.1), dimensions={0}, to_apply=%region_7.8 | reduce | flops 1769472 | bytes 11796484 | tf_op jit(solution)/shard_map/reduce_sum | solution.py:21
  260.5 2.5 multiply_reduce_fusion
  266.0 3.7 all-to-all-start.2
  269.7 3.7 convolution_convert_fusion
  274.5 3.6 all-to-all-start
  278.6 32.1 %all-to-all-done = bf16[8,72,2304]{2,1,0:T(8,128)(2,1)S(1)} async-done(((bf16[8,72,2304]{2,1,0:T(8,128)(2,1)}), bf16[8,72,2304]{2,1,0:T(8,128)(2,1)S(1)}, u32[]{:S(2)}, u32[]{:S(2)}) %all-to-all-start) | async-done | bytes 2654240 | tf_op jit(solution)/shard_map/all_to_all | solution.py:205
  310.7 11.4 %fusion.72 = f32[576,2880]{1,0:T(8,128)S(1)} fusion(bf16[576,2304]{1,0:T(8,128)(2,1)S(1)} %bitcast.155, bf16[2304,2880]{0,1:T(8,128)(2,1)} %bitcast.175), kind=kOutput, calls=%fused_computation.165 | convolution fusion | flops 7644119040 | bytes 22560768 | tf_op jit(solution)/shard_map/dot_general | solution.py:224
  323.4 9.2 %fusion.5 = bf16[576,2304]{1,0:T(8,128)(2,1)} fusion(bf16[1,1440,2304]{2,1,0:T(8,128)(2,1)} %param.30, f32[576,2880]{1,0:T(8,128)S(1)} %multiply_add_fusion), kind=kOutput, calls=%fused_computation.7 | convolution fusion | flops 3828363264 | bytes 16367616 | tf_op jit(solution)/shard_map/dot_general | solution.py:235
  332.6 4.5 %all-to-all-start.3 = ((bf16[8,72,2304]{2,1,0:T(8,128)(2,1)}), bf16[8,72,2304]{2,1,0:T(8,128)(2,1)}, u32[]{:S(2)}, u32[]{:S(2)}) async-start(bf16[8,72,2304]{2,1,0:T(8,128)(2,1)} %bitcast.154), calls=%async_computation.3 | async-start | bytes 5308416 | tf_op jit(solution)/shard_map/all_to_all | solution.py:238
  338.1 3.6 gather_fusion
  342.2 27.5 %all-to-all-done.3 = bf16[8,72,2304]{2,1,0:T(8,128)(2,1)} async-done(((bf16[8,72,2304]{2,1,0:T(8,128)(2,1)}), bf16[8,72,2304]{2,1,0:T(8,128)(2,1)}, u32[]{:S(2)}, u32[]{:S(2)}) %all-to-all-start.3) | async-done | bytes 2654240 | tf_op jit(solution)/shard_map/all_to_all | solution.py:238
  369.7 5.8 %convolution_convert_fusion.1 = bf16[256,2304]{1,0:T(8,128)(2,1)} fusion(f32[256,576]{0,1:T(8,128)S(1)} %select_reduce_fusion, bf16[576,2304]{1,0:T(8,128)(2,1)} %bitcast.66), kind=kOutput, calls=%fused_computation.12 | convolution fusion | flops 4077453312 | bytes 4423680 | tf_op jit(solution)/shard_map/dot_general | solution.py:244
  377.5 3.0 reshape.581
  380.5 6.7 %copy.94 = bf16[6,128,2,576]{1,3,2,0:T(8,128)(2,1)} copy(bf16[6,128,2,576]{3,2,1,0:T(2,128)(2,1)} %reshape.581) | data formatting | bytes 3538944
  387.2 40.8 %all-reduce.2.cloned.1.call-done = bf16[256,2304]{1,0:T(8,128)(2,1)} async-done(((bf16[256,2304]{1,0:T(8,128)(2,1)}), bf16[256,2304]{1,0:T(8,128)(2,1)}) %all-reduce.2.cloned.1.call-update) | async-done | bytes 1179664 | tf_op jit(solution)/shard_map/psum | solution.py:245
  428.0 3.7 add_convert_fusion
  (119 shorter events, 25.6 us)
Async XLA Ops:
  7.2 79.3 %copy-start = (bf16[576,2304]{1,0:T(8,128)(2,1)S(1)}, bf16[576,2304]{1,0:T(8,128)(2,1)}, u32[]{:S(2)}) copy-start(bf16[576,2304]{1,0:T(8,128)(2,1)} %param.27) | copy-start | bytes 7962628
  7.2 44.8 %copy-start.14 = (bf16[2,16,3,576]{3,1,2,0:T(8,128)(2,1)S(1)}, bf16[2,16,3,576]{3,1,2,0:T(8,128)(2,1)}, u32[]{:S(2)}) copy-start(bf16[2,16,3,576]{3,1,2,0:T(8,128)(2,1)} %param.33) | copy-start | bytes 331780
  7.2 56.9 %copy-start.18 = (f32[2304]{0:T(1024)S(1)}, f32[2304]{0:T(1024)}, u32[]{:S(2)}) copy-start(f32[2304]{0:T(1024)} %param.24) | copy-start | bytes 27652
  7.2 63.8 %all-gather.5.cloned.1.call-start = ((), (), s32[]{:S(2)}) async-start(), calls=%async_computation.4 | async-start | bytes 5308416 | tf_op jit(solution)/shard_map/all_gather | solution.py:82
  7.9 76.0 %all-gather.7.cloned.1.call-start = ((), (), s32[]{:S(2)}) async-start(), calls=%async_computation.5 | async-start | bytes 1327104 | tf_op jit(solution)/shard_map/all_gather | solution.py:85
  8.7 247.2 %all-gather.9.cloned.1.call-start = ((), (), s32[]{:S(2)}) async-start(), calls=%async_computation.7 | async-start | bytes 11796480 | tf_op jit(solution)/shard_map/all_gather | solution.py:21
  10.4 53.7 %copy-start.5 = (bf16[256,2304]{1,0:T(8,128)(2,1)S(1)}, bf16[256,2304]{1,0:T(8,128)(2,1)}, u32[]{:S(2)}) copy-start(bf16[256,2304]{1,0:T(8,128)(2,1)} %param.18) | copy-start | bytes 3538948
  71.0 1.4 copy-start.6
  71.0 2.5 slice-start
  73.5 1.3 copy-start.9
  73.5 1.8 copy-start.10
  75.8 1.2 copy-start.8
  78.0 3.4 copy-start.12
  89.0 0.7 copy-start.16
  92.9 173.0 %all-to-all-start.1 = ((bf16[8,1,72]{2,1,0:T(2,128)(2,1)}), bf16[8,1,72]{2,1,0:T(2,128)(2,1)S(1)}, u32[]{:S(2)}, u32[]{:S(2)}) async-start(bf16[8,1,72]{2,1,0:T(2,128)(2,1)} %all_to_all.20), calls=%async_computation.1 | async-start | bytes 8192 | tf_op jit(solution)/shard_map/all_to_all | solution.py:211
  260.5 3.0 copy-start.2
  260.5 2.6 copy-start.7
  260.5 2.6 copy-start.17
  263.0 1.5 slice-start.1
  263.5 1.0 copy-start.3
  266.0 8.5 %all-to-all-start.2 = ((bf16[8,72,16]{1,2,0:T(8,128)(2,1)}), bf16[8,72,16]{1,2,0:T(8,128)(2,1)S(1)}, u32[]{:S(2)}, u32[]{:S(2)}) async-start(bf16[8,72,16]{1,2,0:T(8,128)(2,1)} %copy.92), calls=%async_computation.2 | async-start | bytes 65536 | tf_op jit(solution)/shard_map/all_to_all | solution.py:208
  274.5 36.2 %all-to-all-start = ((bf16[8,72,2304]{2,1,0:T(8,128)(2,1)}), bf16[8,72,2304]{2,1,0:T(8,128)(2,1)S(1)}, u32[]{:S(2)}, u32[]{:S(2)}) async-start(bf16[8,72,2304]{2,1,0:T(8,128)(2,1)} %bitcast.56), calls=%async_computation | async-start | bytes 5308416 | tf_op jit(solution)/shard_map/all_to_all | solution.py:205
  310.7 11.4 %copy-start.11 = (bf16[1,256,2,1440]{1,3,2,0:T(8,128)(2,1)S(1)}, bf16[1,256,2,1440]{1,3,2,0:T(8,128)(2,1)}, u32[]{:S(2)}) copy-start(bf16[1,256,2,1440]{1,3,2,0:T(8,128)(2,1)} %param.31) | copy-start | bytes 4423684
  332.6 5.1 %copy-start.4 = (bf16[256,2304]{1,0:T(8,128)(2,1)S(1)}, bf16[256,2304]{1,0:T(8,128)(2,1)}, u32[]{:S(2)}) copy-start(bf16[256,2304]{1,0:T(8,128)(2,1)} %copy-done.3) | copy-start | bytes 3538948
  332.6 5.1 %copy-start.15 = (bf16[2304,8]{0,1:T(8,128)(2,1)S(1)}, bf16[2304,8]{0,1:T(8,128)(2,1)}, u32[]{:S(2)}) copy-start(bf16[2304,8]{0,1:T(8,128)(2,1)} %param.28) | copy-start | bytes 110596
  332.6 37.1 %all-to-all-start.3 = ((bf16[8,72,2304]{2,1,0:T(8,128)(2,1)}), bf16[8,72,2304]{2,1,0:T(8,128)(2,1)}, u32[]{:S(2)}, u32[]{:S(2)}) async-start(bf16[8,72,2304]{2,1,0:T(8,128)(2,1)} %bitcast.154), calls=%async_computation.3 | async-start | bytes 5308416 | tf_op jit(solution)/shard_map/all_to_all | solution.py:238
  337.1 90.9 %all-reduce.2.cloned.1.call-start = ((), (), s32[]{:S(2)}) async-start(), calls=%async_computation.6 | async-start | bytes 2359296 | tf_op jit(solution)/shard_map/psum | solution.py:245
  369.7 7.0 %copy-start.13 = (bf16[256,9,32]{0,2,1:T(8,128)(2,1)S(1)}, bf16[256,9,32]{0,2,1:T(8,128)(2,1)}, u32[]{:S(2)}) copy-start(bf16[256,9,32]{0,2,1:T(8,128)(2,1)} %copy-done.12) | copy-start | bytes 442372
  380.5 51.2 %copy-start.1 = (bf16[576,2304]{1,0:T(8,128)(2,1)S(1)}, bf16[576,2304]{1,0:T(8,128)(2,1)}, u32[]{:S(2)}) copy-start(bf16[576,2304]{1,0:T(8,128)(2,1)} %param.27) | copy-start | bytes 7962628
Sparse Core Ops, SparseCore 0:
  9.9 42.8 all-gather.4
  54.7 24.0 all-gather.6
  89.1 166.7 all-gather.8
  375.7 52.2 all-reduce.1
